TPU v7x, 128 devices: a whole 4x4x4 slice. The times are simulated.
128 devices in a mesh: req: 4 (over y), wx: 8 (over x, core), wy: 4 (over z).
Axes of the slice: x: 4, y: 4, z: 4, core: 2. Of those that a mesh axis runs over, the one named last changes fastest.
Arguments:
- tokens: bfloat16 [2048, 8192], P('req', 'wy'), may hold values from -6 to 6
- w_in_x: bfloat16 [8192, 8192], P('wy', 'wx'), may hold values from -0.0625 to 0.0625
- w_in_z: bfloat16 [8192, 8192], P('wy', 'wx'), may hold values from -0.0625 to 0.0625
- conv_weight: float32 [4, 8192], P(None, ('wx', 'wy')), may hold values from -3 to 3
- conv_bias: float32 [8192], P(('wx', 'wy')), may hold values from -3 to 3
- w_xproj: bfloat16 [8192, 544], P(('wx', 'wy')), may hold values from -0.0625 to 0.0625
- w_dt: bfloat16 [512, 8192], P(None, ('wx', 'wy')), may hold values from -0.25 to 0.25
- dt_bias: float32 [8192], P(('wx', 'wy')), may hold values from -2 to 0.5
- a_rate: float32 [16, 8192], P(None, ('wx', 'wy')), may hold values from 0.25 to 8
- d_skip: float32 [8192], P(('wx', 'wy')), may hold values from 0.5 to 1.5
- w_out: bfloat16 [8192, 8192], P(('wx', 'wy')), may hold values from -0.0625 to 0.0625
- ssm_state: float32 [512, 16, 8192], P('req', None, ('wx', 'wy')), may hold values from -6 to 6
- conv_state: bfloat16 [512, 3, 8192], P('req', None, ('wx', 'wy')), may hold values from -6 to 6
- accepted: int32 [512], P('req'), may hold values from 0 to 4
- offsets: int32 [512], P('req'), may hold values from 0 to 2044, as said below
Outputs:
- mixed_out: bfloat16 [2048, 8192], P(('req', 'wx', 'wy'))
- new_ssm: float32 [512, 16, 8192], P('req', None, ('wx', 'wy'))
- new_conv: bfloat16 [512, 3, 8192], P('req', None, ('wx', 'wy'))
Inputs may be any that keep to these rules, and one draw needn't show every extreme that they name: Request r owns packed rows offsets[r] to offsets[r] + 3; the requests of the b-th block of 128 requests fill exactly the b-th block of 512 rows, in some order.
All inputs are finite; a program needn't handle non-finite values.
Results may differ from a plain program's by a relative error of at most 0.008.
Values may be sent and summed in bfloat16 or wider, within the bound.
No kernel may reach another device: no remote copies, remote signals or barrier semaphores. Data moves between devices by JAX's collectives and lax.ppermute only.
A program may use at most 128 MiB of HBM per device.

v0:
```python
import jax
import jax.numpy as jnp
from jax import lax
from jax.sharding import PartitionSpec as P

DRAFT = 4


def verify_core(
    draft_x,
    draft_z,
    conv_weight,
    conv_bias,
    w_xproj,
    w_dt,
    dt_bias,
    a_rate,
    d_skip,
    ssm_state,
    conv_state,
    accepted,
):
    requests = draft_x.shape[0]
    drafts = draft_x.shape[1]
    taps = conv_weight.shape[0]
    chans = draft_x.shape[2]
    history = jnp.concatenate([conv_state, draft_x], axis=1)
    conv_sum = jnp.zeros((requests, drafts, chans), jnp.float32) + conv_bias[None, None, :]
    for tap in range(taps):
        conv_sum = (
            conv_sum
            + history[:, tap : tap + drafts].astype(jnp.float32) * conv_weight[tap][None, None, :]
        )
    conv_out = jax.nn.silu(conv_sum).astype(jnp.bfloat16)
    partial_proj = jnp.dot(
        conv_out.reshape(requests * drafts, chans), w_xproj, preferred_element_type=jnp.float32
    )
    projected = lax.psum(partial_proj, ("wx", "wy"))
    rank = w_dt.shape[0]
    nstate = a_rate.shape[0]
    dt_input = projected[:, :rank].astype(jnp.bfloat16)
    b_in = projected[:, rank : rank + nstate].reshape(requests, drafts, nstate)
    c_out = projected[:, rank + nstate :].reshape(requests, drafts, nstate)
    step_size = jax.nn.softplus(
        jnp.dot(dt_input, w_dt, preferred_element_type=jnp.float32) + dt_bias[None, :]
    )
    step_size = step_size.reshape(requests, drafts, chans)
    gate_vals = jax.nn.silu(draft_z.astype(jnp.float32))
    state = ssm_state
    kept = ssm_state
    results = []
    for position in range(drafts):
        xvalue = conv_out[:, position].astype(jnp.float32)
        delta = step_size[:, position]
        decay = jnp.exp(-delta[:, None, :] * a_rate[None, :, :])
        state = decay * state + (delta * xvalue)[:, None, :] * b_in[:, position, :, None]
        kept = jnp.where((accepted == position + 1)[:, None, None], state, kept)
        readout = jnp.sum(c_out[:, position, :, None] * state, axis=1) + d_skip[None, :] * xvalue
        results.append(readout * gate_vals[:, position])
    scanned = jnp.stack(results, axis=1).astype(jnp.bfloat16)
    window = history[:, 0 : taps - 1]
    for shift_by in range(1, drafts + 1):
        window = jnp.where(
            (accepted == shift_by)[:, None, None],
            history[:, shift_by : shift_by + taps - 1],
            window,
        )
    return (scanned, kept, window)


def on_device(
    tokens,
    w_in_x,
    w_in_z,
    conv_weight,
    conv_bias,
    w_xproj,
    w_dt,
    dt_bias,
    a_rate,
    d_skip,
    w_out,
    ssm_state,
    conv_state,
    accepted,
    offsets,
):
    tok_rows = tokens.shape[0]
    chans = w_in_x.shape[1] // lax.axis_size("wy")
    contract = (((0,), (1,)), ((), ()))
    term_x = lax.dot_general(w_in_x, tokens, contract, preferred_element_type=jnp.float32)
    term_z = lax.dot_general(w_in_z, tokens, contract, preferred_element_type=jnp.float32)
    inner_both = lax.psum_scatter(
        jnp.concatenate([term_x, term_z], axis=1), "wy", scatter_dimension=0, tiled=True
    ).astype(jnp.bfloat16)
    x_rows = inner_both[:, :tok_rows].T
    z_rows = inner_both[:, tok_rows:].T
    requests = offsets.shape[0]
    row_index = (
        jnp.remainder(offsets, tok_rows)[:, None] + jnp.arange(DRAFT, dtype=jnp.int32)[None, :]
    )
    flat_index = row_index.reshape(-1)
    draft_x = jnp.take(x_rows, flat_index, axis=0).reshape(requests, DRAFT, chans)
    draft_z = jnp.take(z_rows, flat_index, axis=0).reshape(requests, DRAFT, chans)
    scanned, new_ssm, new_conv = verify_core(
        draft_x,
        draft_z,
        conv_weight,
        conv_bias,
        w_xproj,
        w_dt,
        dt_bias,
        a_rate,
        d_skip,
        ssm_state,
        conv_state,
        accepted,
    )
    packed = (
        jnp.zeros((tok_rows, chans), jnp.bfloat16)
        .at[flat_index]
        .set(scanned.reshape(requests * DRAFT, chans))
    )
    mixed_out = lax.psum_scatter(
        jnp.dot(packed, w_out, preferred_element_type=jnp.float32),
        ("wx", "wy"),
        scatter_dimension=0,
        tiled=True,
    ).astype(jnp.bfloat16)
    return (mixed_out, new_ssm, new_conv)


def solution(mesh):
    placed = (
        P("req", "wy"),
        P("wy", "wx"),
        P("wy", "wx"),
        P(None, ("wx", "wy")),
        P(("wx", "wy")),
        P(("wx", "wy"), None),
        P(None, ("wx", "wy")),
        P(("wx", "wy")),
        P(None, ("wx", "wy")),
        P(("wx", "wy")),
        P(("wx", "wy"), None),
        P("req", None, ("wx", "wy")),
        P("req", None, ("wx", "wy")),
        P("req"),
        P("req"),
    )
    return jax.shard_map(
        on_device,
        mesh=mesh,
        in_specs=placed,
        out_specs=(
            P(("req", "wx", "wy"), None),
            P("req", None, ("wx", "wy")),
            P("req", None, ("wx", "wy")),
        ),
        check_vma=False,
    )
```

profile of v0, /device:TPU:0, one launch (start us, length us, event | category | flops | bytes accessed | tf_op | source)
XLA Modules:
  0.0 338.9 jit_solution(17819976706132863746)
XLA Ops:
  7.2 1.5 copy-done
  8.8 4.7 %fusion.31 = f32[1024,512]{0,1:T(8,128)S(1)} fusion(bf16[512,2048]{1,0:T(8,128)(2,1)S(1)} %copy-done, bf16[2048,1024]{1,0:T(8,128)(2,1)} %param.19), kind=kOutput, calls=%fused_computation.81 | convolution fusion | flops 2147483648 | bytes 8388608 | tf_op jit(solution)/shard_map/dot_general | solution.py:92
  13.4 2.4 fusion.30
  15.8 2.5 pad_maximum_fusion
  19.3 48.7 %reduce-scatter.3.cloned.1.call-done = f32[256,1024]{0,1:T(8,128)} async-done(((f32[1024,1024]{0,1:T(8,128)}), f32[256,1024]{0,1:T(8,128)}) %reduce-scatter.3.cloned.1.call-update) | async-done | bytes 1048592 | tf_op jit(solution)/shard_map/reduce_scatter | solution.py:93
  68.0 1.3 convert_element_type.53
  69.3 2.6 gather_fusion
  71.9 2.6 gather_fusion.1
  74.4 1.2 broadcast_select_fusion
  75.6 0.9 reshape.110
  77.4 2.2 divide_multiply_fusion
  79.9 2.3 fusion.28
  83.0 103.9 %all-reduce.2.cloned.1.call-done = f32[512,544]{0,1:T(8,128)} async-done(((f32[512,544]{0,1:T(8,128)}), f32[512,544]{0,1:T(8,128)}) %all-reduce.2.cloned.1.call-update) | async-done | bytes 1114128 | tf_op jit(solution)/shard_map/psum | solution.py:38
  188.7 2.6 compare_select_fusion
  191.2 1.2 reshape.108
  192.4 1.1 fusion.23
  193.9 1.3 fusion.15
  195.6 5.4 %multiply_reduce_fusion.1 = (f32[128,256]{1,0:T(8,128)S(1)}, f32[128,256]{1,0:T(8,128)S(1)}, f32[128,256]{1,0:T(8,128)S(1)}, f32[128,256]{1,0:T(8,128)S(1)}) fusion(f32[128,16]{1,0:T(8,128)} %bitcast.56, f32[128,256]{1,0:T(8,128)S(1)} %get-tuple-element.27, f32[128,256]{1,0:T(8,128)S(1)} %get-tuple-element.36, f32[128,16]{1,0:T(8,128)S(1)} %bitcast.64, ...), kind=kLoop, calls=%fused_computation.7 | loop fusion | flops 12451840 | bytes 3751936 | tf_op jit(solution)/shard_map/reduce_sum | solution.py:58
  202.1 3.0 scatter_custom_fusion
  205.1 10.3 %fusion.29 = f32[512,8192]{1,0:T(8,128)} fusion(bf16[512,256]{1,0:T(8,128)(2,1)S(1)} %scatter_custom_fusion, bf16[256,8192]{1,0:T(8,128)(2,1)} %param.27), kind=kOutput, calls=%fused_computation.79 | convolution fusion | flops 2147483648 | bytes 21233664 | tf_op jit(solution)/shard_map/dot_general | solution.py:125
  216.4 1.7 fusion.2
  218.1 7.1 %select_select_fusion = f32[128,16,256]{2,1,0:T(8,128)} fusion(f32[128,16,256]{2,1,0:T(8,128)} %param.28, f32[128,16]{1,0:T(8,128)S(1)} %bitcast.55, f32[128,256]{1,0:T(8,128)S(1)} %get-tuple-element.26, f32[128,256]{1,0:T(8,128)} %copy-done.6, f32[128,16]{1,0:T(8,128)} %bitcast.57, f32[128,256]{1,0:T(8,128)S(1)} %get-tuple-element.27, ...), kind=kLoop, calls=%fused_computation.4 | loop fusion | flops 10485760 | bytes 5292544 | tf_op jit(solution)/shard_map/jit(_where)/select_n | solution.py:57
  225.2 105.4 %reduce-scatter.5.cloned.1.call-done = f32[16,8192]{1,0:T(8,128)} async-done(((f32[512,8192]{1,0:T(8,128)}), f32[16,8192]{1,0:T(8,128)}) %reduce-scatter.5.cloned.1.call-update) | async-done | bytes 524304 | tf_op jit(solution)/shard_map/reduce_scatter | solution.py:124
  330.6 1.8 convert_element_type.66
  (60 shorter events, 7.3 us)
Async XLA Ops:
  7.2 1.6 copy-start
  7.2 60.8 %reduce-scatter.3.cloned.1.call-start = ((), (), s32[]{:S(2)}) async-start(), calls=%async_computation.2 | async-start | bytes 5242880 | tf_op jit(solution)/shard_map/reduce_scatter | solution.py:93
  8.8 4.7 %copy-start.12 = (bf16[2048,1024]{1,0:T(8,128)(2,1)S(1)}, bf16[2048,1024]{1,0:T(8,128)(2,1)}, u32[]{:S(2)}) copy-start(bf16[2048,1024]{1,0:T(8,128)(2,1)} %param.18) | copy-start | bytes 12582916
  18.3 0.7 copy-start.14
  18.3 0.9 copy-start.7
  18.3 1.0 copy-start.9
  18.3 168.6 %all-reduce.2.cloned.1.call-start = ((), (), s32[]{:S(2)}) async-start(), calls=%async_computation.3 | async-start | bytes 2228224 | tf_op jit(solution)/shard_map/psum | solution.py:38
  74.4 2.9 copy-start.10
  79.8 108.8 %copy-start.13 = (f32[256]{0:T(256)S(1)}, f32[256]{0:T(256)}, u32[]{:S(2)}) copy-start(f32[256]{0:T(256)} %param.24) | copy-start | bytes 3076
  82.2 248.4 %reduce-scatter.5.cloned.1.call-start = ((), (), s32[]{:S(2)}) async-start(), calls=%async_computation.4 | async-start | bytes 17301504 | tf_op jit(solution)/shard_map/reduce_scatter | solution.py:124
  192.4 2.8 copy-start.8
  193.7 1.8 copy-start.1
  195.2 5.7 %copy-start.4 = (f32[128,256]{1,0:T(8,128)}, f32[128,256]{1,0:T(8,128)S(1)}, u32[]{:S(2)}) copy-start(f32[128,256]{1,0:T(8,128)S(1)} %get-tuple-element.35) | copy-start | bytes 393220
  195.2 5.7 %copy-start.5 = (f32[128,256]{1,0:T(8,128)}, f32[128,256]{1,0:T(8,128)S(1)}, u32[]{:S(2)}) copy-start(f32[128,256]{1,0:T(8,128)S(1)} %get-tuple-element.36) | copy-start | bytes 393220
  195.2 5.7 %copy-start.6 = (f32[128,256]{1,0:T(8,128)}, f32[128,256]{1,0:T(8,128)S(1)}, u32[]{:S(2)}) copy-start(f32[128,256]{1,0:T(8,128)S(1)} %get-tuple-element.37) | copy-start | bytes 393220
  195.6 5.4 %copy-start.2 = (f32[128,4,256]{2,0,1:T(8,128)S(1)}, f32[128,4,256]{2,0,1:T(8,128)}, u32[]{:S(2)}) copy-start(f32[128,4,256]{2,0,1:T(8,128)} %get-tuple-element.48) | copy-start | bytes 1572868
  195.6 5.4 %copy-start.11 = (f32[256]{0:T(256)S(1)}, f32[256]{0:T(256)}, u32[]{:S(2)}) copy-start(f32[256]{0:T(256)} %param.26) | copy-start | bytes 3076
  215.4 1.0 copy-start.3
Sparse Core Ops, SparseCore 0:
  18.4 49.4 reduce-scatter.2
  82.4 104.4 all-reduce.1
  215.5 115.0 reduce-scatter.4
where the time goes:
time: 340 us; the launch traced here: 339 us
  waiting for transfers between devices  258 us (76%)
  other arithmetic  26 us (8%)
  matrix products  22.2 us (7%)
  local copies, waits for them, and re-layouts  18.5 us (5%)
  between operations  14 us (4%)
    reduce_scatter x1, waiting for transfers between devices, on_device(): lax.psum_scatter(jnp.dot(packed, w_out, preferred_element_type=jnp.float3...  105 us
    psum x1, waiting for transfers between devices, verify_core(): projected = lax.psum(partial_proj, ('wx', 'wy'))  104 us
    reduce_scatter x1, waiting for transfers between devices, on_device(): lax.psum_scatter(jnp.concatenate([term_x, term_z], axis=1), 'wy', scatter...  48.7 us
    dot_general x1, matrix products, on_device(): jnp.dot(packed, w_out, preferred_element_type=jnp.float32)  10.3 us
    select_n x1, other arithmetic, verify_core(): kept = jnp.where((accepted == position + 1)[:, None, None], state, kept)  7.08 us
  transfers between devices with their start and end apart: 3, of which 3 were waited for; matrix products, arithmetic and copies ran while one was open for 3% of the time, Pallas kernels for 0%

commit v1 on v0

v1 whole, which is shorter than its diff:
```python
import functools
import math

import jax
import jax.numpy as jnp
from jax import lax
from jax.experimental import pallas as pl
from jax.experimental.pallas import tpu as pltpu
from jax.sharding import PartitionSpec as P

DRAFT = 4
BF = jnp.bfloat16
F32 = jnp.float32
LOG2E = math.log2(math.e)


def params(megabytes=16):
    return pltpu.CompilerParams(vmem_limit_bytes=megabytes * 1024 * 1024)


def cost(flops, nbytes, transcendentals=0):
    return pl.CostEstimate(
        flops=int(flops), bytes_accessed=int(nbytes), transcendentals=int(transcendentals)
    )


def near(value):
    return pltpu.with_memory_space_constraint(value, pltpu.VMEM)


def far(value):
    return pltpu.with_memory_space_constraint(value, pltpu.HBM)


def dot(a, b):
    return jnp.dot(a, b, preferred_element_type=F32)


def dot_rows(a, b):
    return lax.dot_general(a, b, (((1,), (1,)), ((), ())), preferred_element_type=F32)


VM = pl.BlockSpec(memory_space=pltpu.VMEM)
ANY = pl.BlockSpec(memory_space=pl.ANY)
HBM = pl.BlockSpec(memory_space=pltpu.HBM)


def swap_core(value):
    return lax.ppermute(value, "core", [(0, 1), (1, 0)])


def swap_x(value, d):
    return lax.ppermute(value, "x", [(i, i ^ d) for i in range(4)])


def swap_z(value, d):
    return lax.ppermute(value, "wy", [(i, i ^ d) for i in range(4)])


def swap_by_core(value, *ways):
    def index(x, core, z):
        return (x * 2 + core) * 4 + z

    pairs = []
    for x in range(4):
        for core, (axis, d) in enumerate(ways):
            for z in range(4):
                there = (x ^ d, core, z) if axis == "x" else (x, core, z ^ d)
                pairs.append((index(x, core, z), index(*there)))
    return lax.ppermute(value, ("x", "core", "wy"), pairs)


CHUNKS = 4


def multiply(tok, w_ref, w_held, total, sems, tok_ref=None, tok_sems=None):
    depth = w_held.shape[0] // CHUNKS
    slices = [pl.ds(i * depth, depth) for i in range(CHUNKS)]
    copies = []
    for i, here in enumerate(slices):
        copies.append([pltpu.make_async_copy(w_ref.at[here], w_held.at[here], sems.at[i])])
        if tok_ref is not None:
            copies[i].append(
                pltpu.make_async_copy(tok_ref.at[:, here], tok.at[:, here], tok_sems.at[i])
            )
        for copy in copies[i]:
            copy.start()
    for i in range(CHUNKS):
        for copy in copies[i]:
            copy.wait()
        here = slice(i * depth, (i + 1) * depth)
        value = dot(tok[:, here], w_held[here])
        if i == 0:
            total[...] = value
        else:
            total[...] += value


def block_of(total, d):
    chans = total.shape[1] // 4
    return pl.ds(pl.multiple_of((lax.axis_index("wy") ^ d) * chans, chans), chans)


def hand_out(total, send, kept):
    first = 1 + 2 * lax.axis_index("core")
    for out, blocks in ((send, (first, 2)), (kept, (first ^ 2, 0))):
        for i, d in enumerate(blocks):
            out[i] = total[:, block_of(total, d)].astype(out.dtype)


def project_x_kernel(tok_ref, w_ref, send_1, send_2, send_3, kept, tok, w_held, total, sems, tok_sems):
    multiply(tok, w_ref, w_held, total, sems, tok_ref, tok_sems)
    first = 1 + 2 * lax.axis_index("core")
    for out, d in ((send_1, first), (send_2, first ^ 2), (send_3, 2), (kept, 0)):
        out[...] = total[:, block_of(total, d)].astype(out.dtype)


def project_z_kernel(tok, w_ref, after_ref, send, kept, w_held, total, sems):
    del after_ref
    multiply(tok, w_ref, w_held, total, sems)
    hand_out(total, send, kept)


def branch_shapes(rows, weights):
    shape = (2, rows, weights.shape[1] // 4)
    return [pltpu.VMEM(shape, BF), pltpu.VMEM(shape, F32)]


def project_x(tokens, weights):
    rows, depth = tokens.shape
    shape = (rows, weights.shape[1] // 4)
    return pl.pallas_call(
        project_x_kernel,
        in_specs=[HBM, HBM],
        out_specs=[VM] * 5,
        out_shape=[pltpu.VMEM(shape, BF)] * 3
        + [pltpu.VMEM(shape, F32), pltpu.VMEM(tokens.shape, BF)],
        scratch_shapes=[
            pltpu.VMEM(weights.shape, BF),
            pltpu.VMEM((rows, weights.shape[1]), F32),
            pltpu.SemaphoreType.DMA((CHUNKS,)),
            pltpu.SemaphoreType.DMA((CHUNKS,)),
        ],
        compiler_params=params(),
        cost_estimate=cost(2 * rows * depth * weights.shape[1], 12e6),
    )(far(tokens), far(weights))


def project_z(tok, weights, after):
    rows, depth = tok.shape
    return pl.pallas_call(
        project_z_kernel,
        in_specs=[VM, HBM, ANY],
        out_specs=[VM] * 2,
        out_shape=branch_shapes(rows, weights),
        scratch_shapes=[
            pltpu.VMEM(weights.shape, BF),
            pltpu.VMEM((rows, weights.shape[1]), F32),
            pltpu.SemaphoreType.DMA((CHUNKS,)),
        ],
        compiler_params=params(),
        cost_estimate=cost(2 * rows * depth * weights.shape[1], 12e6),
    )(near(tok), far(weights), after)


def first_over_z(send):
    return swap_by_core(send, ("z", 1), ("z", 3))


def second_over_z(kept, got):
    return swap_by_core((kept[0] + got[1].astype(F32)).astype(BF), ("z", 3), ("z", 1))


def exchange_x(x_parts, z_parts):
    send_1, send_2, send_3, kept = x_parts
    got = (
        swap_by_core(send_1, ("z", 1), ("z", 3)),
        swap_by_core(send_2, ("z", 3), ("z", 1)),
        swap_z(send_3, 2),
    )
    *got, z_send, z_kept = lax.optimization_barrier((*got, *z_parts))
    return (kept, *got), [z_send, z_kept]


def assemble(kept_ref, got_ref, last_ref):
    return (kept_ref[1] + got_ref[0].astype(F32) + last_ref[...].astype(F32)).astype(BF)


def column(row_ref):
    size = row_ref.shape[1]
    across = lax.broadcasted_iota(jnp.int32, (size, size), 1)
    down = lax.broadcasted_iota(jnp.int32, (size, size), 0)
    spread = jnp.broadcast_to(row_ref[...].astype(F32), (size, size))
    return jnp.sum(jnp.where(across == down, spread, 0.0), axis=1, keepdims=True).astype(jnp.int32)


def draft_rows(value, first_row, position):
    spots = lax.broadcasted_iota(jnp.int32, (first_row.shape[0], value.shape[0]), 1)
    chosen = jnp.where(spots == first_row + position, 1.0, 0.0).astype(BF)
    return dot(chosen, value)


def conv_kernel(
    off_ref, kept_ref, got_1, got_2, got_3, hist_ref, cw_ref, cb_ref, wx_ref, send_ref, own_ref,
    draft_ref, conv_ref, both
):
    value = add_up(kept_ref[...], [got[...] for got in (got_1, got_2, got_3)]).astype(BF)
    first_row = column(off_ref) % value.shape[0]
    history = [hist_ref[k].astype(F32) for k in range(3)]
    for j in range(DRAFT):
        row = draft_rows(value, first_row, j)
        draft_ref[j] = row.astype(BF)
        history.append(row)
    rank = wx_ref.shape[0] - 32
    narrow = []
    for j in range(DRAFT):
        total = cb_ref[...] + history[j] * cw_ref[0:1]
        for k in range(1, 4):
            total = total + history[j + k] * cw_ref[k : k + 1]
        conv = (total / (1.0 + jnp.exp(-total))).astype(BF)
        conv_ref[j] = conv.astype(F32)
        both[:, j * rank : (j + 1) * rank] = dot_rows(conv, wx_ref[:rank])
        narrow.append(dot_rows(conv, wx_ref[rank:]))
    both[:, DRAFT * rank :] = jnp.concatenate(narrow, axis=1)
    core, me_x = lax.axis_index("core"), lax.axis_index("x")
    half = own_ref.shape[0]
    part = half // 4
    for index, out in ((1 - core, send_ref), (core, own_ref)):
        for d in range(4):
            start = pl.multiple_of(index * half + (me_x ^ d) * part, part)
            out[d * part : (d + 1) * part] = both[pl.ds(start, part)].astype(out.dtype)


def convolve(off_row, terms, hist, conv_weight, conv_bias, w_cols):
    requests = off_row.shape[1]
    chans = conv_weight.shape[1]
    wide = DRAFT * (w_cols.shape[0] - 32) + 128
    operands = (off_row, *terms, hist, conv_weight, conv_bias, w_cols)
    piece = (requests // 2, wide)
    return pl.pallas_call(
        conv_kernel,
        in_specs=[VM] * len(operands),
        out_specs=[VM] * 4,
        out_shape=[
            pltpu.VMEM(piece, BF),
            pltpu.VMEM(piece, F32),
            pltpu.VMEM((DRAFT, requests, chans), BF),
            pltpu.VMEM((DRAFT, requests, chans), F32),
        ],
        scratch_shapes=[pltpu.VMEM((requests, wide), F32)],
        compiler_params=params(),
        cost_estimate=cost(5e8, 4e6, 131072),
    )(*[near(v) for v in operands])


def gate_kernel(
    off_ref, acc_ref, kept_ref, got_ref, last_ref, hist_ref, draft_ref, gate_ref, window_ref
):
    value = assemble(kept_ref, got_ref, last_ref)
    first_row = column(off_ref) % value.shape[0]
    for j in range(DRAFT):
        row = draft_rows(value, first_row, j)
        gate_ref[j] = row / (1.0 + jnp.exp(-row))
    accepted = jnp.broadcast_to(column(acc_ref), draft_ref.shape[1:])
    history = [hist_ref[k].astype(F32) for k in range(3)]
    history += [draft_ref[j].astype(F32) for j in range(DRAFT)]
    for k in range(3):
        window = history[k]
        for shift in range(1, DRAFT + 1):
            window = jnp.where(accepted == shift, history[k + shift], window)
        window_ref[k] = window.astype(BF)


def gates(off_row, acc_row, terms, hist, draft):
    operands = (off_row, acc_row, *terms, hist, draft)
    return pl.pallas_call(
        gate_kernel,
        in_specs=[VM] * len(operands),
        out_specs=[VM] * 2,
        out_shape=[pltpu.VMEM(draft.shape, F32), jax.ShapeDtypeStruct(hist.shape, BF)],
        compiler_params=params(),
        cost_estimate=cost(2.7e8, 2e6, 131072),
    )(*[near(v) for v in operands])


def add_up(value, arrived):
    for one in arrived:
        value = value + one.astype(F32)
    return value


def sum_everywhere(send, own, z_parts, off_row, ssm_state):
    value = own + swap_core(send).astype(F32)
    part = value.shape[0] // 4
    got = [swap_x(value[d * part : (d + 1) * part].astype(BF), d) for d in (1, 3, 2)]
    z_send, z_kept = z_parts
    piece = add_up(value[:part], got)
    piece, z_got = lax.optimization_barrier((piece, first_over_z(z_send)))
    sent = piece.astype(BF)
    got = [swap_z(sent, d) for d in (1, 3, 2)]
    piece = add_up(piece, got).astype(BF)
    got = [swap_x(piece, d) for d in (1, 2, 3)]
    z_last = second_over_z(z_kept, z_got)
    *got, z_last, state, back = lax.optimization_barrier(
        (*got, z_last, *prepare(off_row, ssm_state, sent))
    )
    mine = jnp.concatenate([piece] + got, axis=0)
    return mine, swap_core(mine), (z_kept, z_got, z_last), state, back


PARTS = 4


def prepare_kernel(off_ref, state_ref, after_ref, turned_ref, back_ref, state_in, sems):
    del after_ref
    requests = state_ref.shape[0]
    rows = requests // PARTS
    loads = []
    for p in range(PARTS):
        here = pl.ds(p * rows, rows)
        loads.append(pltpu.make_async_copy(state_ref.at[here], state_in.at[here], sems.at[p]))
        loads[p].start()
    core, me_x, me_z = lax.axis_index("core"), lax.axis_index("x"), lax.axis_index("wy")
    places = back_ref.shape[2]
    place = lax.broadcasted_iota(jnp.int32, (places, requests), 0)
    token = (me_x ^ (place // 64)) * 128 + (me_z ^ ((place // 16) % 4)) * 16 + place % 16
    late = token - jnp.broadcast_to(off_ref[...] % (DRAFT * requests), (places, requests))
    for which, index in enumerate((core, 1 - core)):
        for j in range(DRAFT):
            back_ref[which, j] = jnp.where(late + index * 64 == j, 1.0, 0.0).astype(BF)
    for g in range(requests // 8):
        if (g * 8) % rows == 0:
            loads[g * 8 // rows].wait()
        here = slice(g * 8, g * 8 + 8)
        turned_ref[:, here] = jnp.swapaxes(state_in[here], 0, 1)


def prepare(off_row, state, after):
    requests, nstate, chans = state.shape
    return pl.pallas_call(
        prepare_kernel,
        in_specs=[VM, HBM, ANY],
        out_specs=[VM] * 2,
        out_shape=[
            pltpu.VMEM((nstate, requests, chans), F32),
            pltpu.VMEM((2, DRAFT, DRAFT * requests // 2, requests), BF),
        ],
        scratch_shapes=[pltpu.VMEM(state.shape, F32), pltpu.SemaphoreType.DMA((PARTS,))],
        compiler_params=params(),
        cost_estimate=cost(1e6, 4e6),
    )(near(off_row), far(state), after)


def scan_kernel(
    mine_ref, other_ref, wdt_ref, dtb_ref, a_ref, skip_ref, conv_ref, gate_ref, acc_ref, back_ref,
    state_ref, w_out_ref, w_other_ref, packed_ref, send_ref, kept_ref, w_near_ref, both, delta,
    result, rates, w_sems
):
    rank, chans = wdt_ref.shape
    nstate, requests, _ = state_ref.shape
    core, me_x = lax.axis_index("core"), lax.axis_index("x")
    moves = [
        pltpu.make_async_copy(ref, w_near_ref.at[i], w_sems.at[i])
        for i, ref in enumerate((w_out_ref, w_other_ref))
    ]
    for move in moves:
        move.start()
    half = mine_ref.shape[0]
    part = half // 4
    for index, ref in ((core, mine_ref), (1 - core, other_ref)):
        for d in range(4):
            start = pl.multiple_of(index * half + (me_x ^ d) * part, part)
            both[pl.ds(start, part)] = ref[d * part : (d + 1) * part]
    rates[...] = a_ref[...] * -LOG2E
    for j in range(DRAFT):
        pre = dot(both[:, j * rank : (j + 1) * rank], wdt_ref[...]) + dtb_ref[...]
        delta[j] = jnp.maximum(pre, 0.0) + jnp.log1p(jnp.exp(-jnp.abs(pre)))
    narrow = both[:, DRAFT * rank :].astype(F32)
    accepted_all = column(acc_ref)

    for g in range(requests // 8):
        here = slice(g * 8, g * 8 + 8)
        bc = narrow[here]
        accepted = jnp.broadcast_to(accepted_all[here], (8, chans))
        steps = [delta[j, here] for j in range(DRAFT)]
        convs = [conv_ref[j, here] for j in range(DRAFT)]
        drive = [steps[j] * convs[j] for j in range(DRAFT)]
        read = [skip_ref[...] * convs[j] for j in range(DRAFT)]
        for n in range(nstate):
            rate = rates[n : n + 1]
            state = state_ref[n, here]
            kept = state
            for j in range(DRAFT):
                b = bc[:, 32 * j + n : 32 * j + n + 1]
                c = bc[:, 32 * j + 16 + n : 32 * j + 16 + n + 1]
                state = jnp.exp2(steps[j] * rate) * state + drive[j] * b
                kept = jnp.where(accepted == j + 1, state, kept)
                read[j] = read[j] + c * state
            kept_ref[n, here] = kept
        for j in range(DRAFT):
            result[j, here] = read[j] * gate_ref[j, here]

    for which, out in enumerate((packed_ref, send_ref)):
        total = jnp.zeros(out.shape, F32)
        for j in range(DRAFT):
            total = total + dot(back_ref[which, j], result[j].astype(BF))
        out[...] = total.astype(BF)
    for move in moves:
        move.wait()


def scan(
    mine, other, w_dt, dt_bias, rates, skip, conv, gate, acc_row, back, state, w_out, w_other
):
    nstate, requests, chans = state.shape
    wide = DRAFT * w_dt.shape[0] + 128
    operands = (mine, other, w_dt, dt_bias, rates, skip, conv, gate, acc_row, back, state)
    packed = pltpu.VMEM((DRAFT * requests // 2, chans), BF)
    return pl.pallas_call(
        scan_kernel,
        in_specs=[VM] * len(operands) + [ANY, ANY],
        out_specs=[VM] * 4,
        out_shape=[
            packed,
            packed,
            pltpu.VMEM(state.shape, F32),
            pltpu.VMEM((2, *w_out.shape), BF),
        ],
        scratch_shapes=[
            pltpu.VMEM((requests, wide), BF),
            pltpu.VMEM((DRAFT, requests, chans), F32),
            pltpu.VMEM((DRAFT, requests, chans), F32),
            pltpu.VMEM((nstate, chans), F32),
            pltpu.SemaphoreType.DMA((2,)),
        ],
        compiler_params=params(),
        cost_estimate=cost(1e9, 6e6, 2.2e6),
    )(*[near(v) for v in operands], w_out, w_other)


STREAMS = (
    ("x", 1, 3, (1, 2), (0, 3)),
    ("x", 3, 1, (2, 3), (1, 0)),
    ("z", 1, 3, (1, 2), (0, 3)),
    ("z", 3, 1, (2, 3), (1, 0)),
)


def swap_of(axis):
    return swap_x if axis == "x" else swap_z


def stream_product(s, blocks, mine_ref, other_ref, w_ref):
    axis, part = STREAMS[s][0], w_ref.shape[2] // len(STREAMS)
    columns = slice(s * part, (s + 1) * part)
    value = 0.0
    for ref, w in ((mine_ref, 0), (other_ref, 1)):
        parts = [ref[i] if axis == "x" else ref[:, i] for i in blocks]
        rows = jnp.concatenate([p.reshape(64, p.shape[2]) for p in parts], axis=0)
        value = value + dot(rows, w_ref[w, :, columns])
    return value


def sent_kernel(s, mine_ref, other_ref, w_ref, out_ref):
    out_ref[...] = stream_product(s, STREAMS[s][3], mine_ref, other_ref, w_ref).astype(BF)


def project_sent(s, mine, other, w_near):
    part = w_near.shape[2] // len(STREAMS)
    return pl.pallas_call(
        functools.partial(sent_kernel, s),
        in_specs=[VM] * 3,
        out_specs=VM,
        out_shape=pltpu.VMEM((128, part), BF),
        compiler_params=params(),
        cost_estimate=cost(2 * 128 * 512 * part, 2e6),
    )(near(mine), near(other), near(w_near))


def held_kernel(kept_ref, mine_ref, other_ref, w_ref, *refs):
    outs, (state_ref, turned, sems) = refs[: len(STREAMS)], refs[len(STREAMS) :]
    rows = turned.shape[0] // PARTS
    stores = []
    for p in range(PARTS):
        for g in range(rows // 8):
            here = slice(p * rows + g * 8, p * rows + g * 8 + 8)
            turned[here] = jnp.swapaxes(kept_ref[:, here], 0, 1)
        here = pl.ds(p * rows, rows)
        stores.append(pltpu.make_async_copy(turned.at[here], state_ref.at[here], sems.at[p]))
        stores[p].start()
    for s, out in enumerate(outs):
        out[...] = stream_product(s, STREAMS[s][4], mine_ref, other_ref, w_ref)
    for store in stores:
        store.wait()


def project_held(kept, mine, other, w_near):
    nstate, requests, chans = kept.shape
    part = w_near.shape[2] // len(STREAMS)
    shape = (requests, nstate, chans)
    return pl.pallas_call(
        held_kernel,
        in_specs=[VM] * 4,
        out_specs=[VM] * 4 + [HBM],
        out_shape=[pltpu.VMEM((128, part), F32)] * 4 + [pltpu.HBM(shape, F32)],
        scratch_shapes=[pltpu.VMEM(shape, F32), pltpu.SemaphoreType.DMA((PARTS,))],
        compiler_params=params(),
        cost_estimate=cost(8 * 128 * 512 * part, 8e6),
    )(near(kept), near(mine), near(other), near(w_near))


def add_kernel(forward, held_ref, got_ref, own_ref, pass_ref):
    rows = own_ref.shape[0]
    own, send = (slice(0, rows), slice(rows, None))
    if not forward:
        own, send = send, own
    own_ref[...] = held_ref[own] + got_ref[own].astype(F32)
    pass_ref[...] = (held_ref[send] + got_ref[send].astype(F32)).astype(BF)


def add_arrived(s, held, got):
    shape = (held.shape[0] // 2, held.shape[1])
    return pl.pallas_call(
        functools.partial(add_kernel, STREAMS[s][1] == 1),
        in_specs=[VM] * 2,
        out_specs=[VM] * 2,
        out_shape=[pltpu.VMEM(shape, F32), pltpu.VMEM(shape, BF)],
        compiler_params=params(),
        cost_estimate=cost(held.size, 1e6),
    )(near(held), near(got))


def stage_kernel(own_a, got_a, own_b, got_b, keep_ref, *sends):
    size = keep_ref.shape[0]
    width = own_a.shape[1]
    for own, got, columns in (
        (own_a, got_a, slice(0, width)),
        (own_b, got_b, slice(width, None)),
    ):
        value = own[...] + got[...].astype(F32)
        keep_ref[:, columns] = value[:size]
        for d in range(1, 4):
            sends[d - 1][:, columns] = value[d * size : (d + 1) * size].astype(BF)


def next_stage(own_a, got_a, own_b, got_b):
    shape = (own_a.shape[0] // 4, 2 * own_a.shape[1])
    return pl.pallas_call(
        stage_kernel,
        in_specs=[VM] * 4,
        out_specs=[VM] * 4,
        out_shape=[pltpu.VMEM(shape, F32)] + [pltpu.VMEM(shape, BF)] * 3,
        compiler_params=params(),
        cost_estimate=cost(2 * own_a.size, 1e6),
    )(*[near(v) for v in (own_a, got_a, own_b, got_b)])


def last_kernel(*refs):
    left, right, out_ref = refs[:4], refs[4:8], refs[8]
    width = left[0].shape[1]
    for group, columns in ((left, slice(0, width)), (right, slice(width, None))):
        value = group[0][...]
        for one in group[1:]:
            value = value + one[...].astype(F32)
        out_ref[:, columns] = value.astype(BF)


def last_sum(left, right):
    rows, width = left[0].shape[0], left[0].shape[1] + right[0].shape[1]
    return pl.pallas_call(
        last_kernel,
        in_specs=[VM] * 8,
        out_specs=VM,
        out_shape=jax.ShapeDtypeStruct((rows, width), BF),
        compiler_params=params(),
        cost_estimate=cost(4 * rows * width, 1e6),
    )(*[near(v) for v in (*left, *right)])


def on_device(
    tokens,
    w_in_x,
    w_in_z,
    conv_weight,
    conv_bias,
    w_xproj,
    w_dt,
    dt_bias,
    a_rate,
    d_skip,
    w_out,
    ssm_state,
    conv_state,
    accepted,
    offsets,
):
    off_row, acc_row = offsets[None, :], accepted[None, :]
    hist = jnp.swapaxes(conv_state, 0, 1)

    w_other = swap_core(w_out)
    *x_parts, tok = project_x(tokens, w_in_x)
    z_parts = project_z(tok, w_in_z, x_parts[0])
    x_terms, z_parts = exchange_x(x_parts, z_parts)
    send, own, draft, conv = convolve(
        off_row, x_terms, hist, conv_weight, conv_bias[None, :], jnp.swapaxes(w_xproj, 0, 1)
    )
    z_parts[0], send = lax.optimization_barrier((z_parts[0], send))
    mine, other, z_terms, state, back = sum_everywhere(send, own, z_parts, off_row, ssm_state)
    gate, window = gates(off_row, acc_row, z_terms, hist, draft)
    packed, packed_send, kept, w_near = scan(
        mine,
        other,
        w_dt,
        dt_bias[None, :],
        a_rate,
        d_skip[None, :],
        conv,
        gate,
        acc_row,
        back,
        state,
        w_out,
        w_other,
    )
    new_conv = jnp.swapaxes(window, 0, 1)

    shape = (4, 4, 16, packed.shape[1])
    operands = (packed.reshape(shape), swap_core(packed_send).reshape(shape), w_near)
    got = []
    for s, (axis, one, *_) in enumerate(STREAMS):
        got.append(swap_of(axis)(project_sent(s, *operands), one))
    *helds, new_ssm = project_held(kept, *operands)
    results = []
    for s, (axis, _, two, *_) in enumerate(STREAMS):
        own_rows, passed = add_arrived(s, helds[s], got[s])
        results += [own_rows, swap_of(axis)(passed, two)]
    left, right = next_stage(*results[:4]), next_stage(*results[4:])
    left = (left[0], *[swap_z(left[d], d) for d in (2, 1, 3)])
    right = (right[0], *[swap_x(right[d], d) for d in (2, 1, 3)])
    mixed_out = last_sum(left, right)
    return (mixed_out, new_ssm, new_conv)


def solution(mesh):
    devices = mesh.devices.reshape(4, 4, 2, 4)
    fine = jax.sharding.Mesh(devices, ("req", "x", "core", "wy"))
    every = ("x", "core", "wy")
    wx = ("x", "core")
    placed = (
        P("req", "wy"),
        P("wy", wx),
        P("wy", wx),
        P(None, every),
        P(every),
        P(every, None),
        P(None, every),
        P(every),
        P(None, every),
        P(every),
        P(every, None),
        P("req", None, every),
        P("req", None, every),
        P("req"),
        P("req"),
    )
    return jax.shard_map(
        on_device,
        mesh=fine,
        in_specs=placed,
        out_specs=(
            P(("req", *every), None),
            P("req", None, every),
            P("req", None, every),
        ),
        check_vma=False,
    )
```

time: 340 us -> 103 us (0.30)
  waiting for transfers between devices: 258 us -> 37.7 us
  starting transfers between devices: 0.12 us -> 41.8 us
  other arithmetic: 26 us -> 0.25 us
  Pallas kernels: 0 us -> 22.4 us
  matrix products: 22.2 us -> 0 us
  local copies, waits for them, and re-layouts: 18.5 us -> 0.08 us
  between operations: 14 us -> 0.95 us
    reduce_scatter x2 -> x0, waiting for transfers between devices: 154 us -> none  [the longest x1 105 us: on_device(): lax.psum_scatter(jnp.dot(packed, w_out, preferred_element_type=jnp.float3...]
    psum x1 -> x0, waiting for transfers between devices: 104 us -> none  [verify_core(): projected = lax.psum(partial_proj, ('wx', 'wy'))]
    ppermute x0 -> x32, starting transfers between devices: none -> 41.8 us  [the longest x13 17.7 us: swap_x(): return lax.ppermute(value, 'x', [(i, i ^ d) for i in range(4)])]
    ppermute x0 -> x32, waiting for transfers between devices: none -> 37.7 us  [the longest x13 20.5 us: swap_x(): return lax.ppermute(value, 'x', [(i, i ^ d) for i in range(4)])]
    pallas_call x0 -> x18, Pallas kernels: none -> 22.4 us  [the longest x1 4.28 us: project_x(): pl.pallas_call(project_x_kernel, in_specs=[HBM, HBM], out_specs=[VM] * 5,...]
    dot_general x5 -> x0, matrix products: 22.2 us -> none  [the longest x1 10.3 us: on_device(): jnp.dot(packed, w_out, preferred_element_type=jnp.float32)]
    select_n x6 -> x0, other arithmetic: 10.6 us -> none  [the longest x1 7.08 us: verify_core(): kept = jnp.where((accepted == position + 1)[:, None, None], state, kept)]
    reduce_sum x1 -> x0, other arithmetic: 5.38 us -> none  [verify_core(): jnp.sum(c_out[:, position, :, None] * state, axis=1)]
  transfers between devices with their start and end apart: 3 -> 32, of which waited for: 3 -> 20; matrix products, arithmetic and copies ran while one was open for 3% -> 0% of each run, Pallas kernels for 0% -> 12%
where the time goes in v1:
time: 103 us
  starting transfers between devices  41.8 us (41%)
  waiting for transfers between devices  37.7 us (37%)
  Pallas kernels  22.4 us (22%)
    ppermute x13, waiting for transfers between devices, swap_x(): return lax.ppermute(value, 'x', [(i, i ^ d) for i in range(4)])  20.5 us
    ppermute x13, starting transfers between devices, swap_x(): return lax.ppermute(value, 'x', [(i, i ^ d) for i in range(4)])  17.7 us
    ppermute x11, starting transfers between devices, swap_z(): return lax.ppermute(value, 'wy', [(i, i ^ d) for i in range(4)])  14.3 us
    ppermute x4, waiting for transfers between devices, swap_by_core(): return lax.ppermute(value, ('x', 'core', 'wy'), pairs)  10.6 us
    ppermute x4, starting transfers between devices, swap_by_core(): return lax.ppermute(value, ('x', 'core', 'wy'), pairs)  7.91 us
    pallas_call x1, Pallas kernels, project_x(): pl.pallas_call(project_x_kernel, in_specs=[HBM, HBM], out_specs=[VM] * 5,...  4.28 us
    pallas_call x1, Pallas kernels, scan(): pl.pallas_call(scan_kernel, in_specs=[VM] * len(operands) + [ANY, ANY], o...  4.26 us
    ppermute x11, waiting for transfers between devices, swap_z(): return lax.ppermute(value, 'wy', [(i, i ^ d) for i in range(4)])  4.08 us
  transfers between devices with their start and end apart: 32, of which 20 were waited for; matrix products, arithmetic and copies ran while one was open for 0% of the time, Pallas kernels for 12%

profile of v1, /device:TPU:0, one launch (start us, length us, event | category | flops | bytes accessed | tf_op | source)
XLA Modules:
  0.0 103.1 jit_solution(14007104642860196196)
XLA Ops:
  0.6 4.3 %shard_map.166 = (bf16[512,256]{1,0:T(8,128)(2,1)S(1)}, bf16[512,256]{1,0:T(8,128)(2,1)S(1)}, bf16[512,256]{1,0:T(8,128)(2,1)S(1)}, f32[512,256]{1,0:T(8,128)S(1)}, bf16[512,2048]{1,0:T(8,128)(2,1)S(1)}) custom-call(bf16[512,2048]{1,0:T(8,128)(2,1)} %tok_ref.1, bf16[2048,1024]{1,0:T(8,128)(2,1)} %w_ref.2), custom_call_target="tpu_custom_call" | custom-call | flops 2147483648 | bytes 12000000 | tf_op jit(solution)/shard_map/pallas_call | solution.py:132
  4.9 4.2 %collective-permute-start.1 = (bf16[512,256]{1,0:T(8,128)(2,1)S(1)}, bf16[512,256]{1,0:T(8,128)(2,1)S(1)}, u32[]{:S(2)}, u32[]{:S(2)}) collective-permute-start(bf16[512,256]{1,0:T(8,128)(2,1)S(1)} %get-tuple-element.60), channel_id=1, source_target_pairs={{0,3},{1,2},{2,1},{3,0},{4,5},{5,4},{6,7},{7,6},{8,11},{9,10},{10,... | collective-permute-start | bytes 786440 | tf_op jit(solution)/shard_map/ppermute | solution.py:70
  10.2 4.0 %shard_map.167 = (bf16[2,512,256]{2,1,0:T(8,128)(2,1)S(1)}, f32[2,512,256]{2,1,0:T(8,128)S(1)}) custom-call(bf16[512,2048]{1,0:T(8,128)(2,1)S(1)} %get-tuple-element.62.tok, bf16[2048,1024]{1,0:T(8,128)(2,1)} %w_ref.3, bf16[512,256]{1,0:T(8,128)(2,1)S(1)} %get-tuple-element.59.after_ref), custom_call_target="tpu_custom_call" | custom-call | flops 2147483648 | bytes 12000000 | tf_op jit(solution)/shard_map/pallas_call | solution.py:151
  14.2 6.5 %collective-permute-done.1.got_2 = bf16[512,256]{1,0:T(8,128)(2,1)S(1)} collective-permute-done((bf16[512,256]{1,0:T(8,128)(2,1)S(1)}, bf16[512,256]{1,0:T(8,128)(2,1)S(1)}, u32[]{:S(2)}, u32[]{:S(2)}) %collective-permute-start.1) | collective-permute-done | bytes 262176 | tf_op jit(solution)/shard_map/ppermute | solution.py:70
  24.4 1.6 %collective-permute-start.4 = (bf16[16,2176]{1,0:T(8,128)(2,1)S(1)}, bf16[16,2176]{1,0:T(8,128)(2,1)S(1)}, u32[]{:S(2)}, u32[]{:S(2)}) collective-permute-start(bf16[16,2176]{1,0:T(8,128)(2,1)S(1)} %get-tuple-element.115), channel_id=1, source_target_pairs={{0,8},{8,0},{16,24},{24,16},{1,9},{9,1},{17,25},{25,17},{2,10},{10... | collective-permute-start | bytes 208904 | tf_op jit(solution)/shard_map/ppermute | solution.py:53
  26.0 2.7 %collective-permute-start.6 = (bf16[16,2176]{1,0:T(8,128)(2,1)S(1)}, bf16[16,2176]{1,0:T(8,128)(2,1)S(1)}, u32[]{:S(2)}, u32[]{:S(2)}) collective-permute-start(bf16[16,2176]{1,0:T(8,128)(2,1)S(1)} %get-tuple-element.116), channel_id=1, source_target_pairs={{0,16},{8,24},{16,0},{24,8},{1,17},{9,25},{17,1},{25,9},{2,18},{10... | collective-permute-start | bytes 208904 | tf_op jit(solution)/shard_map/ppermute | solution.py:53
  29.2 3.5 %collective-permute-done.6 = bf16[16,2176]{1,0:T(8,128)(2,1)S(1)} collective-permute-done((bf16[16,2176]{1,0:T(8,128)(2,1)S(1)}, bf16[16,2176]{1,0:T(8,128)(2,1)S(1)}, u32[]{:S(2)}, u32[]{:S(2)}) %collective-permute-start.6) | collective-permute-done | bytes 69664 | tf_op jit(solution)/shard_map/ppermute | solution.py:53
  34.3 4.1 %collective-permute-done.7.got_ref = bf16[2,512,256]{2,1,0:T(8,128)(2,1)S(1)} collective-permute-done((bf16[2,512,256]{2,1,0:T(8,128)(2,1)S(1)}, bf16[2,512,256]{2,1,0:T(8,128)(2,1)S(1)}, u32[]{:S(2)}, u32[]{:S(2)}) %collective-permute-start.7) | collective-permute-done | bytes 524320 | tf_op jit(solution)/shard_map/ppermute | solution.py:70
  38.4 2.4 %collective-permute-start.10 = (bf16[16,2176]{1,0:T(8,128)(2,1)S(1)}, bf16[16,2176]{1,0:T(8,128)(2,1)S(1)}, u32[]{:S(2)}, u32[]{:S(2)}) collective-permute-start(bf16[16,2176]{1,0:T(8,128)(2,1)S(1)} %convert_element_type.44.after_ref), channel_id=1, source_target_pairs={{0,2},{1,3},{2,0},{3,1},{4,6},{5,7},{6,4},{7,5},{8,10},{9,11},{10,... | collective-permute-start | bytes 208904 | tf_op jit(solution)/shard_map/ppermute | solution.py:57
  42.3 2.7 %collective-permute-start.14 = (bf16[512,256]{1,0:T(8,128)(2,1)S(1)}, bf16[512,256]{1,0:T(8,128)(2,1)S(1)}, u32[]{:S(2)}, u32[]{:S(2)}) collective-permute-start(bf16[512,256]{1,0:T(8,128)(2,1)S(1)} %fusion), channel_id=1, source_target_pairs={{0,3},{1,2},{2,1},{3,0},{4,5},{5,4},{6,7},{7,6},{8,11},{9,10},{10,... | collective-permute-start | bytes 786440 | tf_op jit(solution)/shard_map/ppermute | solution.py:70
  46.8 2.8 %collective-permute-start.13 = (bf16[16,2176]{1,0:T(8,128)(2,1)S(1)}, bf16[16,2176]{1,0:T(8,128)(2,1)S(1)}, u32[]{:S(2)}, u32[]{:S(2)}) collective-permute-start(bf16[16,2176]{1,0:T(8,128)(2,1)S(1)} %add_convert_fusion.1), channel_id=1, source_target_pairs={{0,24},{8,16},{16,8},{24,0},{1,25},{9,17},{17,9},{25,1},{2,26},{10... | collective-permute-start | bytes 208904 | tf_op jit(solution)/shard_map/ppermute | solution.py:53
  50.9 1.6 %shard_map.169 = (f32[16,128,256]{2,1,0:T(8,128)S(1)}, bf16[2,4,256,128]{3,2,1,0:T(8,128)(2,1)S(1)}) custom-call(s32[1,128]{1,0:T(1,128)S(1)} %bitcast.25, f32[128,16,256]{2,1,0:T(8,128)} %state_ref.1, bf16[16,2176]{1,0:T(8,128)(2,1)S(1)} %convert_element_type.44.after_ref), custom_call_target="tpu_custom_call" | custom-call | flops 1000000 | bytes 4000000 | tf_op jit(solution)/shard_map/pallas_call | solution.py:340
  52.6 2.8 %collective-permute-done.12 = bf16[16,2176]{1,0:T(8,128)(2,1)S(1)} collective-permute-done((bf16[16,2176]{1,0:T(8,128)(2,1)S(1)}, bf16[16,2176]{1,0:T(8,128)(2,1)S(1)}, u32[]{:S(2)}, u32[]{:S(2)}) %collective-permute-start.12) | collective-permute-done | bytes 69664 | tf_op jit(solution)/shard_map/ppermute | solution.py:53
  57.3 4.3 %shard_map.171 = (bf16[256,256]{1,0:T(8,128)(2,1)S(1)}, bf16[256,256]{1,0:T(8,128)(2,1)S(1)}, f32[16,128,256]{2,1,0:T(8,128)S(1)}, bf16[2,256,8192]{2,1,0:T(8,128)(2,1)S(1)}) custom-call(bf16[64,2176]{1,0:T(8,128)(2,1)S(1)} %pad_maximum_fusion.mine_ref, bf16[64,2176]{1,0:T(8,128)(2,1)S(1)} %collective-permute-done.15.other_ref, ...), custom_call_target="tpu_custom_call" | custom-call | flops 1000000000 | bytes 6000000 | tf_op jit(solution)/shard_map/pallas_call | solution.py:419
  64.0 2.7 %collective-permute-start.20 = (bf16[128,2048]{1,0:T(8,128)(2,1)S(1)}, bf16[128,2048]{1,0:T(8,128)(2,1)S(1)}, u32[]{:S(2)}, u32[]{:S(2)}) collective-permute-start(bf16[128,2048]{1,0:T(8,128)(2,1)S(1)} %shard_map.175), channel_id=1, source_target_pairs={{0,24},{8,16},{16,8},{24,0},{1,25},{9,17},{17,9},{25,1},{2,26},{10... | collective-permute-start | bytes 1572872 | tf_op jit(solution)/shard_map/ppermute | solution.py:53
  68.3 2.8 %collective-permute-start.27 = (bf16[128,2048]{1,0:T(8,128)(2,1)S(1)}, bf16[128,2048]{1,0:T(8,128)(2,1)S(1)}, u32[]{:S(2)}, u32[]{:S(2)}) collective-permute-start(bf16[128,2048]{1,0:T(8,128)(2,1)S(1)} %shard_map.180), channel_id=1, source_target_pairs={{0,3},{1,2},{2,1},{3,0},{4,7},{5,6},{6,5},{7,4},{8,11},{9,10},{10,... | collective-permute-start | bytes 1572872 | tf_op jit(solution)/shard_map/ppermute | solution.py:57
  71.1 2.7 %shard_map.172 = (f32[128,2048]{1,0:T(8,128)S(1)}, f32[128,2048]{1,0:T(8,128)S(1)}, f32[128,2048]{1,0:T(8,128)S(1)}, f32[128,2048]{1,0:T(8,128)S(1)}, f32[128,16,256]{2,1,0:T(8,128)}) custom-call(f32[16,128,256]{2,1,0:T(8,128)S(1)} %get-tuple-element.87.kept_ref, bf16[4,4,16,256]{3,2,1,0:T(8,128)(2,1)S(1)} %bitcast.16, bf16[4,4,16,256]{3,2,1,0:T(8,128)(2,1)S(1)} %bitcast.21, ...), custom_call_target="tpu_custom_call" | custom-call | flops 1073741824 | bytes 8000000 | tf_op jit(solution)/shard_map/pallas_call | solution.py:501
  73.7 3.9 %collective-permute-done.18.got_ref = bf16[128,2048]{1,0:T(8,128)(2,1)S(1)} collective-permute-done((bf16[128,2048]{1,0:T(8,128)(2,1)S(1)}, bf16[128,2048]{1,0:T(8,128)(2,1)S(1)}, u32[]{:S(2)}, u32[]{:S(2)}) %collective-permute-start.18) | collective-permute-done | bytes 524320 | tf_op jit(solution)/shard_map/ppermute | solution.py:53
  80.8 2.5 %collective-permute-start.26 = (bf16[64,2048]{1,0:T(8,128)(2,1)S(1)}, bf16[64,2048]{1,0:T(8,128)(2,1)S(1)}, u32[]{:S(2)}, u32[]{:S(2)}) collective-permute-start(bf16[64,2048]{1,0:T(8,128)(2,1)S(1)} %get-tuple-element.103), channel_id=1, source_target_pairs={{0,3},{1,2},{2,1},{3,0},{4,7},{5,6},{6,5},{7,4},{8,11},{9,10},{10,... | collective-permute-start | bytes 786440 | tf_op jit(solution)/shard_map/ppermute | solution.py:57
  83.8 2.9 %collective-permute-done.19.got_a = bf16[64,2048]{1,0:T(8,128)(2,1)S(1)} collective-permute-done((bf16[64,2048]{1,0:T(8,128)(2,1)S(1)}, bf16[64,2048]{1,0:T(8,128)(2,1)S(1)}, u32[]{:S(2)}, u32[]{:S(2)}) %collective-permute-start.19) | collective-permute-done | bytes 262176 | tf_op jit(solution)/shard_map/ppermute | solution.py:53
  87.3 2.8 %collective-permute-start.22 = (bf16[16,4096]{1,0:T(8,128)(2,1)S(1)}, bf16[16,4096]{1,0:T(8,128)(2,1)S(1)}, u32[]{:S(2)}, u32[]{:S(2)}) collective-permute-start(bf16[16,4096]{1,0:T(8,128)(2,1)S(1)} %get-tuple-element.98), channel_id=1, source_target_pairs={{0,2},{1,3},{2,0},{3,1},{4,6},{5,7},{6,4},{7,5},{8,10},{9,11},{10,... | collective-permute-start | bytes 393224 | tf_op jit(solution)/shard_map/ppermute | solution.py:57
  91.6 2.9 %collective-permute-start.29 = (bf16[16,4096]{1,0:T(8,128)(2,1)S(1)}, bf16[16,4096]{1,0:T(8,128)(2,1)S(1)}, u32[]{:S(2)}, u32[]{:S(2)}) collective-permute-start(bf16[16,4096]{1,0:T(8,128)(2,1)S(1)} %get-tuple-element.108), channel_id=1, source_target_pairs={{0,16},{8,24},{16,0},{24,8},{1,17},{9,25},{17,1},{25,9},{2,18},{10... | collective-permute-start | bytes 393224 | tf_op jit(solution)/shard_map/ppermute | solution.py:53
  94.5 1.7 %collective-permute-done.22.refs_1_ = bf16[16,4096]{1,0:T(8,128)(2,1)S(1)} collective-permute-done((bf16[16,4096]{1,0:T(8,128)(2,1)S(1)}, bf16[16,4096]{1,0:T(8,128)(2,1)S(1)}, u32[]{:S(2)}, u32[]{:S(2)}) %collective-permute-start.22) | collective-permute-done | bytes 131104 | tf_op jit(solution)/shard_map/ppermute | solution.py:57
  99.4 2.9 %collective-permute-done.31.refs_7_ = bf16[16,4096]{1,0:T(8,128)(2,1)S(1)} collective-permute-done((bf16[16,4096]{1,0:T(8,128)(2,1)S(1)}, bf16[16,4096]{1,0:T(8,128)(2,1)S(1)}, u32[]{:S(2)}, u32[]{:S(2)}) %collective-permute-start.31) | collective-permute-done | bytes 131104 | tf_op jit(solution)/shard_map/ppermute | solution.py:53
  (87 shorter events, 27.0 us)
Async XLA Ops:
  4.9 15.8 %collective-permute-start.1 = (bf16[512,256]{1,0:T(8,128)(2,1)S(1)}, bf16[512,256]{1,0:T(8,128)(2,1)S(1)}, u32[]{:S(2)}, u32[]{:S(2)}) collective-permute-start(bf16[512,256]{1,0:T(8,128)(2,1)S(1)} %get-tuple-element.60), channel_id=1, source_target_pairs={{0,3},{1,2},{2,1},{3,0},{4,5},{5,4},{6,7},{7,6},{8,11},{9,10},{10,... | collective-permute-start | bytes 786440 | tf_op jit(solution)/shard_map/ppermute | solution.py:70
  9.2 11.6 %collective-permute-start.2 = (bf16[512,256]{1,0:T(8,128)(2,1)S(1)}, bf16[512,256]{1,0:T(8,128)(2,1)S(1)}, u32[]{:S(2)}, u32[]{:S(2)}) collective-permute-start(bf16[512,256]{1,0:T(8,128)(2,1)S(1)} %get-tuple-element.61), channel_id=1, source_target_pairs={{0,2},{1,3},{2,0},{3,1},{4,6},{5,7},{6,4},{7,5},{8,10},{9,11},{10,... | collective-permute-start | bytes 786440 | tf_op jit(solution)/shard_map/ppermute | solution.py:57
  9.2 11.6 %collective-permute-start = (bf16[512,256]{1,0:T(8,128)(2,1)S(1)}, bf16[512,256]{1,0:T(8,128)(2,1)S(1)}, u32[]{:S(2)}, u32[]{:S(2)}) collective-permute-start(bf16[512,256]{1,0:T(8,128)(2,1)S(1)} %get-tuple-element.59.after_ref), channel_id=1, source_target_pairs={{0,1},{1,0},{2,3},{3,2},{4,7},{5,6},{6,5},{7,4},{8,9},{9,8},{10,11... | collective-permute-start | bytes 786440 | tf_op jit(solution)/shard_map/ppermute | solution.py:70
  10.1 47.1 %collective-permute-start.16 = (bf16[256,8192]{1,0:T(8,128)(2,1)S(1)}, bf16[256,8192]{1,0:T(8,128)(2,1)S(1)}, u32[]{:S(2)}, u32[]{:S(2)}) collective-permute-start(bf16[256,8192]{1,0:T(8,128)(2,1)S(1)} %copy-done), channel_id=1, source_target_pairs={{0,4},{4,0},{1,5},{5,1},{2,6},{6,2},{3,7},{7,3},{8,12},{12,8},{9,1... | collective-permute-start | bytes 12582920 | tf_op jit(solution)/shard_map/ppermute | solution.py:49
  26.0 6.7 %collective-permute-start.6 = (bf16[16,2176]{1,0:T(8,128)(2,1)S(1)}, bf16[16,2176]{1,0:T(8,128)(2,1)S(1)}, u32[]{:S(2)}, u32[]{:S(2)}) collective-permute-start(bf16[16,2176]{1,0:T(8,128)(2,1)S(1)} %get-tuple-element.116), channel_id=1, source_target_pairs={{0,16},{8,24},{16,0},{24,8},{1,17},{9,25},{17,1},{25,9},{2,18},{10... | collective-permute-start | bytes 208904 | tf_op jit(solution)/shard_map/ppermute | solution.py:53
  29.2 9.2 %collective-permute-start.7 = (bf16[2,512,256]{2,1,0:T(8,128)(2,1)S(1)}, bf16[2,512,256]{2,1,0:T(8,128)(2,1)S(1)}, u32[]{:S(2)}, u32[]{:S(2)}) collective-permute-start(bf16[2,512,256]{2,1,0:T(8,128)(2,1)S(1)} %get-tuple-element.72), channel_id=1, source_target_pairs={{0,1},{1,0},{2,3},{3,2},{4,7},{5,6},{6,5},{7,4},{8,9},{9,8},{10,11... | collective-permute-start | bytes 1572872 | tf_op jit(solution)/shard_map/ppermute | solution.py:70
  38.4 6.6 %collective-permute-start.10 = (bf16[16,2176]{1,0:T(8,128)(2,1)S(1)}, bf16[16,2176]{1,0:T(8,128)(2,1)S(1)}, u32[]{:S(2)}, u32[]{:S(2)}) collective-permute-start(bf16[16,2176]{1,0:T(8,128)(2,1)S(1)} %convert_element_type.44.after_ref), channel_id=1, source_target_pairs={{0,2},{1,3},{2,0},{3,1},{4,6},{5,7},{6,4},{7,5},{8,10},{9,11},{10,... | collective-permute-start | bytes 208904 | tf_op jit(solution)/shard_map/ppermute | solution.py:57
  42.3 13.1 %collective-permute-start.14 = (bf16[512,256]{1,0:T(8,128)(2,1)S(1)}, bf16[512,256]{1,0:T(8,128)(2,1)S(1)}, u32[]{:S(2)}, u32[]{:S(2)}) collective-permute-start(bf16[512,256]{1,0:T(8,128)(2,1)S(1)} %fusion), channel_id=1, source_target_pairs={{0,3},{1,2},{2,1},{3,0},{4,5},{5,4},{6,7},{7,6},{8,11},{9,10},{10,... | collective-permute-start | bytes 786440 | tf_op jit(solution)/shard_map/ppermute | solution.py:70
  46.8 5.8 %collective-permute-start.13 = (bf16[16,2176]{1,0:T(8,128)(2,1)S(1)}, bf16[16,2176]{1,0:T(8,128)(2,1)S(1)}, u32[]{:S(2)}, u32[]{:S(2)}) collective-permute-start(bf16[16,2176]{1,0:T(8,128)(2,1)S(1)} %add_convert_fusion.1), channel_id=1, source_target_pairs={{0,24},{8,16},{16,8},{24,0},{1,25},{9,17},{17,9},{25,1},{2,26},{10... | collective-permute-start | bytes 208904 | tf_op jit(solution)/shard_map/ppermute | solution.py:53
  49.6 5.8 %collective-permute-start.12 = (bf16[16,2176]{1,0:T(8,128)(2,1)S(1)}, bf16[16,2176]{1,0:T(8,128)(2,1)S(1)}, u32[]{:S(2)}, u32[]{:S(2)}) collective-permute-start(bf16[16,2176]{1,0:T(8,128)(2,1)S(1)} %add_convert_fusion.1), channel_id=1, source_target_pairs={{0,16},{8,24},{16,0},{24,8},{1,17},{9,25},{17,1},{25,9},{2,18},{10... | collective-permute-start | bytes 208904 | tf_op jit(solution)/shard_map/ppermute | solution.py:53
  49.6 5.8 %collective-permute-start.11 = (bf16[16,2176]{1,0:T(8,128)(2,1)S(1)}, bf16[16,2176]{1,0:T(8,128)(2,1)S(1)}, u32[]{:S(2)}, u32[]{:S(2)}) collective-permute-start(bf16[16,2176]{1,0:T(8,128)(2,1)S(1)} %add_convert_fusion.1), channel_id=1, source_target_pairs={{0,8},{8,0},{16,24},{24,16},{1,9},{9,1},{17,25},{25,17},{2,10},{10... | collective-permute-start | bytes 208904 | tf_op jit(solution)/shard_map/ppermute | solution.py:53
  63.5 14.2 %collective-permute-start.18 = (bf16[128,2048]{1,0:T(8,128)(2,1)S(1)}, bf16[128,2048]{1,0:T(8,128)(2,1)S(1)}, u32[]{:S(2)}, u32[]{:S(2)}) collective-permute-start(bf16[128,2048]{1,0:T(8,128)(2,1)S(1)} %shard_map.173), channel_id=1, source_target_pairs={{0,8},{8,0},{16,24},{24,16},{1,9},{9,1},{17,25},{25,17},{2,10},{10... | collective-permute-start | bytes 1572872 | tf_op jit(solution)/shard_map/ppermute | solution.py:53
  64.0 15.4 %collective-permute-start.20 = (bf16[128,2048]{1,0:T(8,128)(2,1)S(1)}, bf16[128,2048]{1,0:T(8,128)(2,1)S(1)}, u32[]{:S(2)}, u32[]{:S(2)}) collective-permute-start(bf16[128,2048]{1,0:T(8,128)(2,1)S(1)} %shard_map.175), channel_id=1, source_target_pairs={{0,24},{8,16},{16,8},{24,0},{1,25},{9,17},{17,9},{25,1},{2,26},{10... | collective-permute-start | bytes 1572872 | tf_op jit(solution)/shard_map/ppermute | solution.py:53
  67.1 13.6 %collective-permute-start.25 = (bf16[128,2048]{1,0:T(8,128)(2,1)S(1)}, bf16[128,2048]{1,0:T(8,128)(2,1)S(1)}, u32[]{:S(2)}, u32[]{:S(2)}) collective-permute-start(bf16[128,2048]{1,0:T(8,128)(2,1)S(1)} %shard_map.178), channel_id=1, source_target_pairs={{0,1},{1,0},{2,3},{3,2},{4,5},{5,4},{6,7},{7,6},{8,9},{9,8},{10,11... | collective-permute-start | bytes 1572872 | tf_op jit(solution)/shard_map/ppermute | solution.py:57
  68.3 15.1 %collective-permute-start.27 = (bf16[128,2048]{1,0:T(8,128)(2,1)S(1)}, bf16[128,2048]{1,0:T(8,128)(2,1)S(1)}, u32[]{:S(2)}, u32[]{:S(2)}) collective-permute-start(bf16[128,2048]{1,0:T(8,128)(2,1)S(1)} %shard_map.180), channel_id=1, source_target_pairs={{0,3},{1,2},{2,1},{3,0},{4,7},{5,6},{6,5},{7,4},{8,11},{9,10},{10,... | collective-permute-start | bytes 1572872 | tf_op jit(solution)/shard_map/ppermute | solution.py:57
  77.7 8.9 %collective-permute-start.19 = (bf16[64,2048]{1,0:T(8,128)(2,1)S(1)}, bf16[64,2048]{1,0:T(8,128)(2,1)S(1)}, u32[]{:S(2)}, u32[]{:S(2)}) collective-permute-start(bf16[64,2048]{1,0:T(8,128)(2,1)S(1)} %get-tuple-element.93), channel_id=1, source_target_pairs={{0,24},{8,16},{16,8},{24,0},{1,25},{9,17},{17,9},{25,1},{2,26},{10... | collective-permute-start | bytes 786440 | tf_op jit(solution)/shard_map/ppermute | solution.py:53
  79.5 7.7 %collective-permute-start.21 = (bf16[64,2048]{1,0:T(8,128)(2,1)S(1)}, bf16[64,2048]{1,0:T(8,128)(2,1)S(1)}, u32[]{:S(2)}, u32[]{:S(2)}) collective-permute-start(bf16[64,2048]{1,0:T(8,128)(2,1)S(1)} %get-tuple-element.96), channel_id=1, source_target_pairs={{0,8},{8,0},{16,24},{24,16},{1,9},{9,1},{17,25},{25,17},{2,10},{10... | collective-permute-start | bytes 786440 | tf_op jit(solution)/shard_map/ppermute | solution.py:53
  80.8 10.7 %collective-permute-start.26 = (bf16[64,2048]{1,0:T(8,128)(2,1)S(1)}, bf16[64,2048]{1,0:T(8,128)(2,1)S(1)}, u32[]{:S(2)}, u32[]{:S(2)}) collective-permute-start(bf16[64,2048]{1,0:T(8,128)(2,1)S(1)} %get-tuple-element.103), channel_id=1, source_target_pairs={{0,3},{1,2},{2,1},{3,0},{4,7},{5,6},{6,5},{7,4},{8,11},{9,10},{10,... | collective-permute-start | bytes 786440 | tf_op jit(solution)/shard_map/ppermute | solution.py:57
  83.5 8.0 %collective-permute-start.28 = (bf16[64,2048]{1,0:T(8,128)(2,1)S(1)}, bf16[64,2048]{1,0:T(8,128)(2,1)S(1)}, u32[]{:S(2)}, u32[]{:S(2)}) collective-permute-start(bf16[64,2048]{1,0:T(8,128)(2,1)S(1)} %get-tuple-element.106), channel_id=1, source_target_pairs={{0,1},{1,0},{2,3},{3,2},{4,5},{5,4},{6,7},{7,6},{8,9},{9,8},{10,11... | collective-permute-start | bytes 786440 | tf_op jit(solution)/shard_map/ppermute | solution.py:57
  87.3 8.8 %collective-permute-start.22 = (bf16[16,4096]{1,0:T(8,128)(2,1)S(1)}, bf16[16,4096]{1,0:T(8,128)(2,1)S(1)}, u32[]{:S(2)}, u32[]{:S(2)}) collective-permute-start(bf16[16,4096]{1,0:T(8,128)(2,1)S(1)} %get-tuple-element.98), channel_id=1, source_target_pairs={{0,2},{1,3},{2,0},{3,1},{4,6},{5,7},{6,4},{7,5},{8,10},{9,11},{10,... | collective-permute-start | bytes 393224 | tf_op jit(solution)/shard_map/ppermute | solution.py:57
  90.1 7.1 %collective-permute-start.23 = (bf16[16,4096]{1,0:T(8,128)(2,1)S(1)}, bf16[16,4096]{1,0:T(8,128)(2,1)S(1)}, u32[]{:S(2)}, u32[]{:S(2)}) collective-permute-start(bf16[16,4096]{1,0:T(8,128)(2,1)S(1)} %get-tuple-element.99), channel_id=1, source_target_pairs={{0,1},{1,0},{2,3},{3,2},{4,5},{5,4},{6,7},{7,6},{8,9},{9,8},{10,11... | collective-permute-start | bytes 393224 | tf_op jit(solution)/shard_map/ppermute | solution.py:57
  90.7 6.6 %collective-permute-start.24 = (bf16[16,4096]{1,0:T(8,128)(2,1)S(1)}, bf16[16,4096]{1,0:T(8,128)(2,1)S(1)}, u32[]{:S(2)}, u32[]{:S(2)}) collective-permute-start(bf16[16,4096]{1,0:T(8,128)(2,1)S(1)} %get-tuple-element.100), channel_id=1, source_target_pairs={{0,3},{1,2},{2,1},{3,0},{4,7},{5,6},{6,5},{7,4},{8,11},{9,10},{10,... | collective-permute-start | bytes 393224 | tf_op jit(solution)/shard_map/ppermute | solution.py:57
  91.6 6.7 %collective-permute-start.29 = (bf16[16,4096]{1,0:T(8,128)(2,1)S(1)}, bf16[16,4096]{1,0:T(8,128)(2,1)S(1)}, u32[]{:S(2)}, u32[]{:S(2)}) collective-permute-start(bf16[16,4096]{1,0:T(8,128)(2,1)S(1)} %get-tuple-element.108), channel_id=1, source_target_pairs={{0,16},{8,24},{16,0},{24,8},{1,17},{9,25},{17,1},{25,9},{2,18},{10... | collective-permute-start | bytes 393224 | tf_op jit(solution)/shard_map/ppermute | solution.py:53
  96.1 6.2 %collective-permute-start.31 = (bf16[16,4096]{1,0:T(8,128)(2,1)S(1)}, bf16[16,4096]{1,0:T(8,128)(2,1)S(1)}, u32[]{:S(2)}, u32[]{:S(2)}) collective-permute-start(bf16[16,4096]{1,0:T(8,128)(2,1)S(1)} %get-tuple-element.110), channel_id=1, source_target_pairs={{0,24},{8,16},{16,8},{24,0},{1,25},{9,17},{17,9},{25,1},{2,26},{10... | collective-permute-start | bytes 393224 | tf_op jit(solution)/shard_map/ppermute | solution.py:53
  (19 other events, 153.9 us)
